TPU v7x, 128 devices: a whole 4x4x4 slice. The times are simulated.
128 devices in a mesh: section: 4 (over z), tensor: 8 (over y, x_lo), dp: 4 (over x_hi, core).
Axes of the slice: x: 4 (x_hi: 2, x_lo: 2; x = x_hi * 2 + x_lo), y: 4, z: 4, core: 2. Of those that a mesh axis runs over, the one named last changes fastest.
Arguments:
- queries: bfloat16 [4, 4, 3584, 8192], P('section', 'dp', None, 'tensor')
- grad_out: bfloat16 [4, 4, 3584, 8192], P('section', 'dp', None, 'tensor'), may hold values from -6 to 6
- tiles: bfloat16 [4, 512, 8192], P('dp', ('section', 'tensor')), may hold values from -6 to 6
- key_value_matrix: bfloat16 [4, 8192, 8, 2, 128], P('section', None, 'tensor'), may hold values from -0.0625 to 0.0625
- gate: float32 [4], P('section'), may hold values from 0.3 to 1.5
- tile_count: int32 [4], P('dp'), may hold values from 256 to 512, as said below
Outputs:
- query_grad: bfloat16 [4, 4, 3584, 8192], P('section', 'dp', None, 'tensor')
- tile_grad: bfloat16 [4, 512, 8192], P('dp', ('section', 'tensor'))
- weight_gradient: bfloat16 [4, 8192, 8, 2, 128], P('section', None, 'tensor')
Inputs may be any that keep to these rules, and one draw needn't show every extreme that they name: `tile_count`: each report has 256 to 512 valid tiles, and one report has all 512.
All inputs are finite; a program needn't handle non-finite values.
Results may differ from a plain program's by a relative error of at most 0.039.
The roundings to bfloat16 on the way count: a program that leaves them out, or rounds other values in their place, can miss the bound.
Values may be sent and summed in bfloat16 or wider, within the bound.
A program may use at most 192 MiB of HBM per device.

v0:
```python
import functools
import heapq

import jax
import jax.numpy as jnp
from jax import lax
from jax.experimental import pallas as pl
from jax.experimental.pallas import tpu as pltpu
from jax.sharding import PartitionSpec as P

F32, BF = jnp.float32, jnp.bfloat16
SC = 128 ** -0.5
LOG2E = 1.4426950408889634


def dg(a, b, ca, cb):
    return lax.dot_general(a, b, (((ca,), (cb,)), ((), ())), preferred_element_type=F32)

MESH = pl.DeviceIdType.MESH
SIZES = {"z": 4, "y": 4, "x": 2}
AX = "zyx"

def gather_plan(parts, latency=0.3):
    def dirs(a):
        return (1,) if SIZES[a] == 2 else (1, -1)
    def shift(u, a, s):
        u = list(u); n = AX.index(a); u[n] = (u[n] - s) % SIZES[a]
        return tuple(u)
    def sends_of(p, u, via):
        order, _, flip = parts[p]
        out = []
        if via is not None:
            a, s = via
            k = order.index(a)
            if SIZES[a] == 4 and u[AX.index(a)] in (1, 3):
                d = -1 if u[AX.index(a)] == 1 else 1
                par = (sum(u[AX.index(b)] for b in order[:k]) + flip) % 2
                if (d == 1) == (par == 0):
                    out.append((p, u, a, d))
            rest = order[k + 1:]
        else:
            rest = order
        for a in rest:
            for d in dirs(a):
                out.append((p, u, a, d))
        return out
    free = {}
    heap = []
    cnt = 0
    def push(t, sends):
        nonlocal cnt
        for (p, u, a, d) in sends:
            t0 = max(t, free.get((a, d), 0.0))
            t1 = t0 + parts[p][1]
            free[(a, d)] = t1
            cnt += 1
            heapq.heappush(heap, (t1 + latency, cnt, p, shift(u, a, d), (a, d)))
    init = [s for p in range(len(parts)) for s in sends_of(p, (0, 0, 0), None)]
    push(0.0, init)
    events, last = [], 0.0
    while heap:
        t, _, p, u, via = heapq.heappop(heap)
        s = sends_of(p, u, via)
        events.append((t, p, u, s))
        push(t, s)
        last = t
    for p in range(len(parts)):
        got = sorted(u for _, q, u, _ in events if q == p)
        full = 1
        for a in parts[p][0]:
            full *= SIZES[a]
        assert len(got) == len(set(got)) == full - 1
    return init, events, last, dict(free)

def place():
    z = lax.axis_index("section"); t = lax.axis_index("tensor")
    return z, t // 2, t % 2

def neighbour(zyx, a, d):
    z, y, x = zyx
    if a == "z":
        return {"section": (z + d) % 4}
    if a == "y":
        return {"tensor": ((y + d) % 4) * 2 + x}
    return {"tensor": y * 2 + (1 - x)}

def uidx(u):
    return u[0] * 8 + u[1] * 2 + u[2]

def row_of(zyx, u):
    z, y, x = zyx
    return ((z + u[0]) % 4) * 8 + ((y + u[1]) % 4) * 2 + (x + u[2]) % 2

def greet(zyx):
    bar = pltpu.get_barrier_semaphore()
    ns = [("x", 1), ("y", 1), ("y", -1), ("z", 1), ("z", -1)]
    for a, d in ns:
        pl.semaphore_signal(bar, inc=1, device_id=neighbour(zyx, a, d), device_id_type=MESH)
    pl.semaphore_wait(bar, len(ns))

PARTS = {4: [("xyz", 0.6875, 0), ("xzy", 0.6875, 0), ("yzx", 0.3125, 0), ("zyx", 0.3125, 1)]}
COLS = {4: [(0, 2816), (2816, 2816), (5632, 1280), (6912, 1280)]}

def ag_kernel(np_, tiles_ref, w_ref, kv_ref, out_ref, buf, raw, wide, acc, send_sem, recv_sem, loc_sem):
    zyx = place()
    dp = lax.axis_index("dp")
    init, events, _, _ = gather_plan(PARTS[np_])
    cols = COLS[np_]
    mine = row_of(zyx, (0, 0, 0))
    loc = pltpu.make_async_copy(tiles_ref.at[0], buf.at[pl.ds(pl.multiple_of(mine * 16, 16), 16)], loc_sem.at[0])
    loc.start()
    load_w = pltpu.make_async_copy(w_ref, raw, loc_sem.at[1])
    load_w.start()
    greet(zyx)
    started = []

    def view(ref, p, u):
        return ref.at[pl.ds(pl.multiple_of(row_of(zyx, u) * 16, 16), 16), pl.ds(*cols[p])]

    def start(p, u, a, d):
        n = AX.index(a)
        v = list(u)
        v[n] = (v[n] - d) % SIZES[a]
        src = tiles_ref.at[0, :, pl.ds(*cols[p])] if u == (0, 0, 0) else view(buf, p, u)
        c = pltpu.make_async_remote_copy(
            src_ref=src, dst_ref=view(buf, p, u),
            send_sem=send_sem.at[len(started)], recv_sem=recv_sem.at[p * 32 + uidx(v)],
            device_id=neighbour(zyx, a, d), device_id_type=MESH)
        c.start()
        started.append(c)

    def wait(p, u):
        v = view(buf, p, u)
        pltpu.make_async_copy(v, v, recv_sem.at[p * 32 + uidx(u)]).wait()

    for s in init:
        start(*s)
    done = 0
    for n, (_, p, u, sends) in enumerate(events):
        wait(p, u)
        for s in sends:
            start(*s)
        if n % 12 == 5 and done < 8:
            if done == 0:
                load_w.wait()
            rows = pl.ds(done * 1024, 1024)
            wide[rows] = raw[rows].reshape(1024, 256)
            done += 1
    assert done == 8
    loc.wait()
    outs = []
    for k in range(2):
        c = pltpu.make_async_copy(
            buf.at[:, pl.ds(pl.multiple_of((dp ^ k) * 2048, 2048), 2048)], out_ref.at[k], loc_sem.at[2 + k])
        c.start()
        outs.append(c)
    acc[...] = jnp.zeros_like(acc)

    def project(j, _):
        at = pl.ds(pl.multiple_of(j * 1024, 1024), 1024)
        acc[...] += dg(buf[:, at], wide[at], 1, 0)
        return 0

    lax.fori_loop(0, 8, project, 0)
    kv_ref[...] = acc[...].astype(BF)
    for c in started:
        c.wait_send()
    for c in outs:
        c.wait()


def nsends(np_):
    init, events, _, _ = gather_plan(PARTS[np_])
    return len(init) + sum(len(e[3]) for e in events)


def gather_and_project(tiles, weight, np_=4, cid=0):
    dma = pltpu.SemaphoreType.DMA
    hbm = pl.BlockSpec(memory_space=pl.ANY)
    return pl.pallas_call(
        functools.partial(ag_kernel, np_),
        in_specs=[hbm, hbm],
        out_specs=[pl.BlockSpec(memory_space=pltpu.VMEM), hbm],
        out_shape=[jax.ShapeDtypeStruct((512, 256), BF), jax.ShapeDtypeStruct((2, 512, 2048), BF)],
        scratch_shapes=[
            pltpu.VMEM((512, 8192), BF), pltpu.VMEM((8192, 2, 128), BF), pltpu.VMEM((8192, 256), BF),
            pltpu.VMEM((512, 256), F32), dma((nsends(np_),)), dma((np_ * 32,)), dma((4,))],
        compiler_params=pltpu.CompilerParams(
            vmem_limit_bytes=60 * 2**20, collective_id=cid, has_side_effects=True),
    )(tiles, weight)


def attention_rows(lay, sub, f, cnt, q_ref, g_ref, kv_ref, dq_ref, ka, va, opt=""):
    k = kv_ref[:, :128]; v = kv_ref[:, 128:]
    J = k.shape[0]; R = q_ref.shape[0]; H = J // 2
    ax = 0 if lay == "T" else 1
    valid = lax.broadcasted_iota(jnp.int32, (H, 1) if ax == 0 else (1, H), ax) + H < cnt
    items = [(h, r) for r in range(R // sub) for h in range(8)]
    def first(it):
        h, r = it
        rs = pl.ds(r * sub, sub); c = pl.ds(h * 128, 128)
        q = q_ref[rs, c]; g = (f * g_ref[rs, c].astype(F32)).astype(BF)
        if lay == "T": return q, g, dg(k, q, 1, 1), dg(v, g, 1, 1)
        return q, g, dg(q, k, 1, 1), dg(g, v, 1, 1)
    def mid(q, g, s, dp):
        if ax == 0: s = jnp.concatenate([s[:H], jnp.where(valid, s[H:], -jnp.inf)], axis=0)
        else: s = jnp.concatenate([s[:, :H], jnp.where(valid, s[:, H:], -jnp.inf)], axis=1)
        m = jnp.max(s, axis=ax, keepdims=True)
        e = jnp.exp2((s - m) * (SC * LOG2E))
        inv = 1.0 / jnp.sum(e, axis=ax, keepdims=True)
        delta = jnp.sum(e * dp, axis=ax, keepdims=True) * inv
        ph = (e * inv).astype(BF)
        ds = ((e * (inv * SC)) * (dp - delta)).astype(BF)
        return ds, ph
    def last(it, q, g, ds, ph):
        h, r = it
        o = (pl.ds(r * sub, sub), pl.ds(h * 128, 128))
        if lay == "T":
            dq_ref[o] = dg(k, ds, 0, 0).T.astype(BF)
            ka[...] += dg(ds, q, 1, 0); va[...] += dg(ph, g, 1, 0)
        else:
            dq_ref[o] = dg(ds, k, 1, 0).astype(BF)
            ka[...] += dg(q, ds, 0, 0); va[...] += dg(g, ph, 0, 0)
    nxt = first(items[0]); prev = None
    for n, it in enumerate(items):
        cur = nxt
        if n + 1 < len(items): nxt = first(items[n + 1])
        if prev is not None: last(*prev)
        b = mid(*cur)
        prev = (it, cur[0], cur[1], *b)
    last(*prev)


def background_plan(steps, unit_us=4.0, start_us=12.0, step_us=3.5):
    parts = [("zy", 1.0, 0), ("yz", 1.0, 1)]
    init, events, _, _ = gather_plan(parts, latency=0.7)
    per_step = [[] for _ in range(steps)]
    for t, p, u, sends in events:
        n = int((start_us + t * unit_us) / step_us) + 1
        per_step[min(n, steps - 1)].append((p, u, sends))
    return init, per_step


def count_sends(init, per_step):
    return len(init) + sum(len(e[2]) for b in per_step for e in b)


def hello_all(zyx):
    z, y, x = zyx
    dp = lax.axis_index("dp")
    peers = [{"section": (z + d) % 4} for d in (1, 2, 3)]
    peers += [{"tensor": ((y + d) % 4) * 2 + x} for d in (1, 2, 3)]
    peers += [{"tensor": y * 2 + (1 - x)}]
    peers += [{"dp": dp ^ k} for k in (1, 2, 3)]
    for d in peers:
        pl.semaphore_signal(pltpu.get_barrier_semaphore(), inc=1, device_id=d, device_id_type=MESH)


def all_said_hello():
    pl.semaphore_wait(pltpu.get_barrier_semaphore(), 10)


def attention_kernel(steps, cnt_ref, fac_ref, q_ref, g_ref, kv_ref, tiles_ref, all_ref, w_ref,
                     dq_ref, pair_ref, others_ref, wz_ref, ka, va,
                     send_sem, recv_sem, swap_send, swap_recv, e_send, e_recv, w_send, w_recv, c_send, c_recv, x_send, x_recv):
    i = pl.program_id(0)
    zyx = place()
    z, y, x = zyx
    dp = lax.axis_index("dp")
    core = dp % 2
    init, per_step = background_plan(steps)
    started = []

    def rows(u):
        return pl.ds(pl.multiple_of(row_of(zyx, u) * 16, 16), 16)

    def pair_rows(u):
        at = ((z + u[0]) % 4) * 8 + ((y + u[1]) % 4) * 2
        return pl.ds(pl.multiple_of(at * 16, 32), 32)

    def quarter(d):
        return pl.ds(pl.multiple_of(d * 2048, 2048), 2048)

    def part_copy(p, u, a, d, at=None):
        if at is None:
            at = len(started)
            started.append((p, u, a, d, at))
        n = AX.index(a)
        v = list(u)
        v[n] = (v[n] - d) % SIZES[a]
        c = pltpu.make_async_remote_copy(
            src_ref=others_ref.at[p, pair_rows(u)], dst_ref=others_ref.at[p, pair_rows(u)],
            send_sem=send_sem.at[at], recv_sem=recv_sem.at[p * 32 + uidx(v)],
            device_id=neighbour(zyx, a, d), device_id_type=MESH)
        return c

    def landed(ref, sem):
        pltpu.make_async_copy(ref, ref, sem).wait()

    def swap(p):
        return pltpu.make_async_remote_copy(
            src_ref=tiles_ref.at[0, :, quarter(dp ^ (2 + p))], dst_ref=others_ref.at[p, rows((0, 0, 0))],
            send_sem=swap_send.at[p], recv_sem=swap_recv.at[p], device_id={"dp": dp ^ (2 + p)}, device_id_type=MESH)

    def across(p, far=0):
        u = others_ref.at[p, rows((0, 0, far))]
        return pltpu.make_async_remote_copy(
            src_ref=u, dst_ref=u, send_sem=e_send.at[p], recv_sem=e_recv.at[p],
            device_id=neighbour(zyx, "x", 1), device_id_type=MESH)

    def w_copy(h, d):
        t = ((z, y)[h] + d) % 4
        dev = {"section": t} if h == 0 else {"tensor": t * 2 + x}
        return pltpu.make_async_remote_copy(
            src_ref=w_ref.at[pl.ds(pl.multiple_of(h * 4096 + t * 1024 + core * 512, 512), 512)],
            dst_ref=wz_ref.at[h, 4 - d, pl.ds(pl.multiple_of(core * 512, 512), 512)],
            send_sem=w_send.at[h, d - 1], recv_sem=w_recv.at[h, 3 - d], device_id=dev, device_id_type=MESH)

    def half(h, k, c):
        return wz_ref.at[h, k, pl.ds(pl.multiple_of(c * 512, 512), 512)]

    def c_copy(h, k):
        return pltpu.make_async_remote_copy(
            src_ref=half(h, k, core), dst_ref=half(h, k, core), send_sem=c_send.at[h, k - 1],
            recv_sem=c_recv.at[h, k - 1], device_id={"dp": dp ^ 1}, device_id_type=MESH)

    def x_copy():
        return pltpu.make_async_remote_copy(
            src_ref=all_ref.at[1], dst_ref=others_ref.at[2],
            send_sem=x_send, recv_sem=x_recv, device_id={"dp": dp ^ 1}, device_id_type=MESH)

    @pl.when(i == 0)
    def _():
        ka[...] = jnp.zeros_like(ka)
        va[...] = jnp.zeros_like(va)
        hello_all(zyx)

    for n in range(1, steps):
        def batch(n=n):
            if n == 1:
                all_said_hello()
                for p in (0, 1):
                    swap(p).start()
                for d in (1, 3):
                    for h in (0, 1):
                        w_copy(h, d).start()
                x_copy().start()
            if n == 2:
                for p in (0, 1):
                    landed(others_ref.at[p, rows((0, 0, 0))], swap_recv.at[p])
                    across(p).start()
            if n == 3:
                for p in (0, 1):
                    landed(others_ref.at[p, rows((0, 0, 1))], e_recv.at[p])
                for s in init:
                    part_copy(*s).start()
            for p, u, sends in per_step[n]:
                landed(others_ref.at[p, pair_rows(u)], recv_sem.at[p * 32 + uidx(u)])
                for s in sends:
                    part_copy(*s).start()
            if n == 9:
                for h in (0, 1):
                    w_copy(h, 2).start()
            if n == steps - 1:
                for k in (1, 3, 2):
                    for h in (0, 1):
                        landed(half(h, k, core), w_recv.at[h, k - 1])
                        c_copy(h, k).start()
        assert n >= 4 or not per_step[n]
        if n in (1, 2, 3, 9, steps - 1) or per_step[n]:
            pl.when(i == n)(batch)

    attention_rows("L", q_ref.shape[0], fac_ref[0], cnt_ref[0], q_ref, g_ref, kv_ref, dq_ref, ka, va)

    @pl.when(i == steps - 1)
    def _():
        pair_ref[:, :128] = ka[...].T.astype(BF)
        pair_ref[:, 128:] = va[...].T.astype(BF)
        for s in started:
            part_copy(*s).wait_send()
        for p in (0, 1):
            swap(p).wait_send()
        for p in (0, 1):
            across(p).wait_send()
        for h in (0, 1):
            for d in (1, 2, 3):
                w_copy(h, d).wait_send()
            for k in (1, 2, 3):
                c_copy(h, k).wait_send()
                landed(half(h, k, 1 - core), c_recv.at[h, k - 1])
        x_copy().wait()


def attention(q, g, kv, cnt, fac, tiles, every_tile, weight, R=256):
    n = q.shape[0]
    steps = n // R
    hbm = pl.BlockSpec(memory_space=pl.ANY)
    dma = pltpu.SemaphoreType.DMA
    return pl.pallas_call(
        functools.partial(attention_kernel, steps),
        grid=(steps,),
        in_specs=[pl.BlockSpec(memory_space=pltpu.SMEM)] * 2 + [
            pl.BlockSpec((R, 1024), lambda i: (i, 0)),
            pl.BlockSpec((R, 1024), lambda i: (i, 0)),
            pl.BlockSpec((512, 256), lambda i: (0, 0)), hbm, hbm, hbm],
        out_specs=[pl.BlockSpec((R, 1024), lambda i: (i, 0)), pl.BlockSpec((512, 256), lambda i: (0, 0)), hbm, hbm],
        out_shape=[jax.ShapeDtypeStruct((n, 1024), BF), jax.ShapeDtypeStruct((512, 256), BF),
                   jax.ShapeDtypeStruct((3, 512, 2048), BF), jax.ShapeDtypeStruct((2, 4, 1024, 2, 128), BF)],
        scratch_shapes=[pltpu.VMEM((128, 512), F32)] * 2 + [
            dma((count_sends(*background_plan(steps)),)), dma((64,)), dma((2,)), dma((2,)), dma((2,)), dma((2,)),
            dma((2, 3)), dma((2, 3)), dma((2, 3)), dma((2, 3)), dma, dma],
        compiler_params=pltpu.CompilerParams(
            vmem_limit_bytes=60 * 2**20, dimension_semantics=("arbitrary",), collective_id=1, has_side_effects=True),
    )(cnt, fac, q, g, kv, tiles, every_tile, weight)


def tail_kernel(pair_ref, others_ref, all_ref, wz_ref, w_ref, tg_ref, wg_ref,
                pza, pzb, pr, gq, wv, wq, tp, rs, own, xs, xr, zs,
                l_sem, p_send, p_recv, s_send, s_recv, f_send, f_recv, g_send, g_recv, h_send, h_recv,
                y_send, y_recv, x_send, x_recv, z_send, z_recv, o_sem):
    zyx = place()
    z, y, x = zyx
    dp = lax.axis_index("dp")

    def remote(src, dst, ss, rs_, dev):
        return pltpu.make_async_remote_copy(
            src_ref=src, dst_ref=dst, send_sem=ss, recv_sem=rs_, device_id=dev, device_id_type=MESH)

    loads = [pltpu.make_async_copy(pair_ref, pr.at[0], l_sem.at[0]),
             pltpu.make_async_copy(all_ref.at[0], gq.at[0], l_sem.at[1]),
             pltpu.make_async_copy(others_ref.at[2], gq.at[1], l_sem.at[2]),
             pltpu.make_async_copy(others_ref.at[0], gq.at[2], l_sem.at[3]),
             pltpu.make_async_copy(others_ref.at[1], gq.at[3], l_sem.at[4])]
    for h in range(2):
        at = pl.multiple_of(h * 4096 + (z, y)[h] * 1024, 1024)
        loads.append(pltpu.make_async_copy(w_ref.at[pl.ds(at, 1024)], wv.at[h, 0], l_sem.at[5 + h * 4]))
        for k in (1, 2, 3):
            loads.append(pltpu.make_async_copy(wz_ref.at[h, k], wv.at[h, k], l_sem.at[5 + h * 4 + k]))
    for c in loads:
        c.start()
    hello_all(zyx)
    all_said_hello()
    sends = []

    def go(c):
        c.start()
        sends.append(c)
        return c

    to2 = go(remote(pair_ref, pr.at[2], p_send.at[0], p_recv.at[0], {"dp": dp ^ 2}))
    to1 = go(remote(pair_ref, pr.at[1], p_send.at[1], p_recv.at[1], {"dp": dp ^ 1}))
    def peer(h, t):
        return {"section": t} if h == 0 else {"tensor": t * 2 + x}

    def part(ref, h, e):
        return ref.at[pl.ds(2 * e, 2)] if h == 0 else ref.at[:, pl.ds(2 * e, 2)]

    at = (z, y)
    pz = (pza, pzb)
    for e in range(2):
        for d in (1, 3, 2):
            for h in range(2):
                go(remote(part(pair_ref, h, e), pz[h].at[3 - d, e], s_send.at[h, d - 1, e], s_recv.at[h, 3 - d, e],
                          peer(h, (at[h] + d) % 4)))
    to2.wait_recv()
    to3 = go(remote(pr.at[2], pr.at[3], f_send, f_recv, {"dp": dp ^ 1}))
    to1.wait_recv()
    for c in loads[:5]:
        c.wait()
    to3.wait_recv()

    def wrows(d, j):
        return wg_ref.at[pl.ds(pl.multiple_of(d * 2048 + j * 512, 512), 512)]

    g2, g1, outs = [], [], []

    def wgrad(j):
        cols = pl.ds(j * 512, 512)
        acc = dg(pr[0].reshape(512, 256), gq[0, :, cols], 0, 0)
        for s in (1, 2, 3):
            acc = acc + dg(pr[s].reshape(512, 256), gq[s, :, cols], 0, 0)
        wq[cols] = acc.T.astype(BF).reshape(512, 2, 128)
        g2.append(go(remote(wq.at[cols], wrows(dp, j), g_send.at[0, j], g_recv.at[0, j], {"dp": dp ^ 2})))
        g1.append(go(remote(wq.at[cols], wrows(dp, j), g_send.at[1, j], g_recv.at[1, j], {"dp": dp ^ 1})))
        outs.append(pltpu.make_async_copy(wq.at[cols], wrows(dp, j), o_sem.at[2 + j]))
        outs[-1].start()

    g3 = []

    def pass_on(j):
        g2[j].wait_recv()
        g3.append(go(remote(wrows(dp ^ 2, j), wrows(dp ^ 2, j), h_send.at[j], h_recv.at[j], {"dp": dp ^ 1})))

    for c in loads[5:]:
        c.wait()
    for e in range(2):
        wgrad(2 * e)
        wgrad(2 * e + 1)
        for h in range(2):
            for k in range(3):
                pltpu.make_async_copy(pz[h].at[k, e], pz[h].at[k, e], s_recv.at[h, k, e]).wait()

            def tile_part(j, _, h=h, e=e):
                cols = pl.ds(pl.multiple_of(j * 512, 512), 512)
                rows = part(pr.at[0], h, e)[...].reshape(256, 256)
                acc = dg(rows, wv[h, 0, cols].reshape(512, 256), 1, 1)
                for k in range(3):
                    acc = acc + dg(pz[h][k, e].reshape(256, 256), wv[h, k + 1, cols].reshape(512, 256), 1, 1)
                t = acc.astype(BF)
                for a in range(2 if h == 0 else 4):
                    for b in range(4 if h == 0 else 2):
                        n = (a * 4 + b) if h == 0 else (a * 2 + b)
                        block = t[n * 32:(n + 1) * 32].reshape(2, 16, 512)
                        if h == 0:
                            tp[h, e, b, :, a, :, cols] = block
                        else:
                            tp[h, e, a, :, b, :, cols] = block
                return 0

            lax.fori_loop(0, 2, tile_part, 0)
            for d in (1, 3, 2):
                t = (at[1 - h] + d) % 4
                go(remote(tp.at[h, e, t], rs.at[h, e, 3 - d], y_send.at[h, e, d - 1], y_recv.at[h, e, 3 - d],
                          peer(1 - h, t)))

    for e in range(2):
        for h in range(2):
            for s in range(3):
                pltpu.make_async_copy(rs.at[h, e, s], rs.at[h, e, s], y_recv.at[h, e, s]).wait()
            for f in range(2):
                tot = tp[h, e, at[1 - h], f].astype(F32)
                for s in range(3):
                    tot = tot + rs[h, e, s, f].astype(F32)
                own[h, e, f] = tot
            xs[h, e] = own[h, e, 1 - x].astype(BF)
            go(remote(xs.at[h, e], xr.at[h, e], x_send.at[h, e], x_recv.at[h, e], {"tensor": y * 2 + (1 - x)}))
        pass_on(e)

    for h in range(2):
        for e in range(2):
            pltpu.make_async_copy(xr.at[h, e], xr.at[h, e], x_recv.at[h, e]).wait()
            zs[h, pl.ds(2 * e, 2)] = (own[h, e, x] + xr[h, e].astype(F32)).astype(BF)
        cols = pl.ds(pl.multiple_of(h * 4096 + at[h] * 1024, 1024), 1024)
        for d in (1, 3, 2):
            t = (at[h] + d) % 4
            go(remote(zs.at[h, t], tg_ref.at[:, cols], z_send.at[h, d - 1], z_recv.at[h, 3 - d], peer(h, t)))
        c = pltpu.make_async_copy(zs.at[h, at[h]], tg_ref.at[:, cols], o_sem.at[h])
        c.start()
        outs.append(c)

    pass_on(2)
    pass_on(3)
    for j in range(4):
        g1[j].wait_recv()
        g3[j].wait_recv()
    for h in range(2):
        for d in (1, 2, 3):
            s = (at[h] + d) % 4
            v = tg_ref.at[:, pl.ds(pl.multiple_of(h * 4096 + s * 1024, 1024), 1024)]
            pltpu.make_async_copy(v, v, z_recv.at[h, d - 1]).wait()
    for c in outs:
        c.wait()
    for c in sends:
        c.wait_send()


def tail(pair, others, every_tile, wz, weight):
    hbm = pl.BlockSpec(memory_space=pl.ANY)
    dma = pltpu.SemaphoreType.DMA
    return pl.pallas_call(
        tail_kernel,
        in_specs=[pl.BlockSpec(memory_space=pltpu.HBM)] * 5,
        out_specs=[hbm] * 2,
        out_shape=[jax.ShapeDtypeStruct((16, 8192), BF), jax.ShapeDtypeStruct((8192, 2, 128), BF)],
        scratch_shapes=[
            pltpu.VMEM((3, 2, 2, 4, 32, 256), BF), pltpu.VMEM((3, 2, 4, 2, 32, 256), BF), pltpu.VMEM((4, 4, 4, 32, 256), BF), pltpu.VMEM((4, 512, 2048), BF),
            pltpu.VMEM((2, 4, 1024, 2, 128), BF), pltpu.VMEM((2048, 2, 128), BF),
            pltpu.VMEM((2, 2, 4, 2, 2, 16, 1024), BF), pltpu.VMEM((2, 2, 3, 2, 2, 16, 1024), BF),
            pltpu.VMEM((2, 2, 2, 2, 16, 1024), F32), pltpu.VMEM((2, 2, 2, 16, 1024), BF),
            pltpu.VMEM((2, 2, 2, 16, 1024), BF), pltpu.VMEM((2, 4, 16, 1024), BF),
            dma((13,)), dma((2,)), dma((2,)), dma((2, 3, 2)), dma((2, 3, 2)), dma, dma, dma((2, 4)), dma((2, 4)), dma((4,)), dma((4,)),
            dma((2, 2, 3)), dma((2, 2, 3)), dma((2, 2)), dma((2, 2)), dma((2, 3)), dma((2, 3)), dma((6,))],
        compiler_params=pltpu.CompilerParams(
            vmem_limit_bytes=50 * 2**20, collective_id=2, has_side_effects=True),
    )(pair, others, every_tile, wz, weight)


def local(queries, grad_out, tiles, key_value_matrix, gate, tile_count):
    packed = key_value_matrix.reshape(8192, 2, 128)
    kv, quarters = gather_and_project(tiles, packed)
    query_grad, pair, others, wz = attention(
        queries[0, 0], grad_out[0, 0], kv, tile_count, jnp.tanh(gate), tiles, quarters, packed
    )
    tile_grad, weight_gradient = tail(pair.reshape(4, 4, 32, 256), others, quarters, wz, packed)
    return (query_grad[None, None], tile_grad[None], weight_gradient.reshape(1, 8192, 1, 2, 128))


def solution(mesh):
    return jax.shard_map(
        local,
        mesh=mesh,
        in_specs=(
            P("section", "dp", None, "tensor"),
            P("section", "dp", None, "tensor"),
            P("dp", ("section", "tensor"), None),
            P("section", None, "tensor", None, None),
            P("section"),
            P("dp"),
        ),
        out_specs=(
            P("section", "dp", None, "tensor"),
            P("dp", ("section", "tensor"), None),
            P("section", None, "tensor", None, None),
        ),
        check_vma=False,
    )
```

profile of v0, /device:TPU:0, one launch (start us, length us, event | category | flops | bytes accessed | tf_op | source)
XLA Modules:
  0.0 172.5 jit_solution(855678925395224738)
XLA Ops:
  0.6 55.7 %shard_map.85 = (bf16[512,256]{1,0:T(8,128)(2,1)}, bf16[2,512,2048]{2,1,0:T(8,128)(2,1)}) custom-call(bf16[1,16,8192]{2,1,0:T(8,128)(2,1)} %tiles_ref.3, bf16[8192,2,128]{2,1,0:T(2,128)(2,1)} %bitcast.11), custom_call_target="tpu_custom_call" | custom-call | tf_op jit(solution)/shard_map/pallas_call | solution.py:180
  57.6 59.3 %shard_map.86 = (bf16[3584,1024]{1,0:T(8,128)(2,1)}, bf16[512,256]{1,0:T(8,128)(2,1)}, bf16[3,512,2048]{2,1,0:T(8,128)(2,1)}, bf16[2,4,1024,2,128]{4,3,2,1,0:T(2,128)(2,1)}) custom-call(s32[1]{0:T(128)S(6)} %copy.14.cnt_ref, f32[1]{0:T(128)S(6)} %tanh.3.fac_ref, bf16[3584,1024]{1,0:T(8,128)(2,1)} %bitcast.15, bf16[3584,1024]{1,0:T(8,128)(2,1)} %bitcast.16, ...), custom_call_target="tpu_custom_call" | custom-call | tf_op jit(solution)/shard_map/pallas_call | solution.py:399
  116.9 0.0 copy-start
  116.9 0.9 copy-done
  117.9 0.0 copy-start.1
  117.9 47.6 %shard_map.87 = (bf16[16,8192]{1,0:T(8,128)(2,1)S(1)}, bf16[8192,2,128]{2,1,0:T(2,128)(2,1)}) custom-call(bf16[4,4,32,256]{3,2,1,0:T(8,128)(2,1)S(1)} %bitcast.9, bf16[3,512,2048]{2,1,0:T(8,128)(2,1)} %get-tuple-element.15.others_ref, bf16[2,512,2048]{2,1,0:T(8,128)(2,1)} %get-tuple-element.12.all_ref, ...), custom_call_target="tpu_custom_call" | custom-call | tf_op jit(solution)/shard_map/pallas_call | solution.py:570
  165.5 0.0 copy-done.1
  165.5 0.0 copy-start.2
  165.5 3.7 %copy.15 = bf16[1,1,3584,1024]{3,2,1,0:T(8,128)(2,1)} copy(bf16[1,1,3584,1024]{3,2,1,0:T(8,128)(2,1)S(1)} %bitcast.14) | data formatting | bytes 14680064
  169.3 0.7 copy.16
  170.0 0.5 copy-done.2
  170.5 2.0 %copy.17 = bf16[1,8192,1,2,128]{4,3,2,1,0:T(2,128)(2,1)} copy(bf16[1,8192,1,2,128]{4,3,2,1,0:T(2,128)(2,1)S(1)} %bitcast.17) | data formatting | bytes 8388608
Async XLA Ops:
  116.9 1.0 copy-start
  117.9 47.7 %copy-start.1 = (bf16[3584,1024]{1,0:T(8,128)(2,1)S(1)}, bf16[3584,1024]{1,0:T(8,128)(2,1)}, u32[]{:S(2)}) copy-start(bf16[3584,1024]{1,0:T(8,128)(2,1)} %get-tuple-element.13) | copy-start | bytes 22020100
  165.5 4.9 %copy-start.2 = (bf16[8192,2,128]{2,1,0:T(2,128)(2,1)S(1)}, bf16[8192,2,128]{2,1,0:T(2,128)(2,1)}, u32[]{:S(2)}) copy-start(bf16[8192,2,128]{2,1,0:T(2,128)(2,1)} %get-tuple-element.18) | copy-start | bytes 12582916
where the time goes:
time: 173 us; the launch traced here: 172 us
  Pallas kernels  163 us (94%)
  local copies, waits for them, and re-layouts  7.88 us (5%)
  between operations  2.01 us (1%)
    pallas_call x1, Pallas kernels, attention(): pl.pallas_call(functools.partial(attention_kernel, steps), grid=(steps,),...  59.3 us
    pallas_call x1, Pallas kernels, gather_and_project(): pl.pallas_call(functools.partial(ag_kernel, np_), in_specs=[hbm, hbm], ou...  55.7 us
    pallas_call x1, Pallas kernels, tail(): pl.pallas_call(tail_kernel, in_specs=[pl.BlockSpec(memory_space=pltpu.HBM...  47.6 us
    unnamed x9, local copies, waits for them, and re-layouts  7.88 us

commit v1 on v0

--- a/solution.py
+++ b/solution.py
@@ -104,7 +104,7 @@
 def ag_kernel(np_, tiles_ref, w_ref, kv_ref, out_ref, buf, raw, wide, acc, send_sem, recv_sem, loc_sem):
     zyx = place()
     dp = lax.axis_index("dp")
-    init, events, _, _ = gather_plan(PARTS[np_])
+    init, events, _, _ = gather_plan(PARTS[np_], latency=0.7)
     cols = COLS[np_]
     mine = row_of(zyx, (0, 0, 0))
     loc = pltpu.make_async_copy(tiles_ref.at[0], buf.at[pl.ds(pl.multiple_of(mine * 16, 16), 16)], loc_sem.at[0])
@@ -170,7 +170,7 @@
 
 
 def nsends(np_):
-    init, events, _, _ = gather_plan(PARTS[np_])
+    init, events, _, _ = gather_plan(PARTS[np_], latency=0.7)
     return len(init) + sum(len(e[3]) for e in events)
 
 

time: 173 us -> 171 us (0.988)
  Pallas kernels: 163 us -> 160 us
where the time goes in v1:
time: 171 us; the launch traced here: 170 us
  Pallas kernels  160 us (94%)
  local copies, waits for them, and re-layouts  7.88 us (5%)
  between operations  2.01 us (1%)
    pallas_call x1, Pallas kernels, attention(): pl.pallas_call(functools.partial(attention_kernel, steps), grid=(steps,),...  58.1 us
    pallas_call x1, Pallas kernels, gather_and_project(): pl.pallas_call(functools.partial(ag_kernel, np_), in_specs=[hbm, hbm], ou...  54.4 us
    pallas_call x1, Pallas kernels, tail(): pl.pallas_call(tail_kernel, in_specs=[pl.BlockSpec(memory_space=pltpu.HBM...  47.9 us
    unnamed x9, local copies, waits for them, and re-layouts  7.88 us

profile of v1, /device:TPU:0, one launch (start us, length us, event | category | flops | bytes accessed | tf_op | source)
XLA Modules:
  0.0 170.3 jit_solution(4688594496488484934)
XLA Ops:
  0.6 54.4 %shard_map.85 = (bf16[512,256]{1,0:T(8,128)(2,1)}, bf16[2,512,2048]{2,1,0:T(8,128)(2,1)}) custom-call(bf16[1,16,8192]{2,1,0:T(8,128)(2,1)} %tiles_ref.3, bf16[8192,2,128]{2,1,0:T(2,128)(2,1)} %bitcast.11), custom_call_target="tpu_custom_call" | custom-call | tf_op jit(solution)/shard_map/pallas_call | solution.py:180
  56.4 58.1 %shard_map.86 = (bf16[3584,1024]{1,0:T(8,128)(2,1)}, bf16[512,256]{1,0:T(8,128)(2,1)}, bf16[3,512,2048]{2,1,0:T(8,128)(2,1)}, bf16[2,4,1024,2,128]{4,3,2,1,0:T(2,128)(2,1)}) custom-call(s32[1]{0:T(128)S(6)} %copy.14.cnt_ref, f32[1]{0:T(128)S(6)} %tanh.3.fac_ref, bf16[3584,1024]{1,0:T(8,128)(2,1)} %bitcast.15, bf16[3584,1024]{1,0:T(8,128)(2,1)} %bitcast.16, ...), custom_call_target="tpu_custom_call" | custom-call | tf_op jit(solution)/shard_map/pallas_call | solution.py:399
  114.5 0.0 copy-start
  114.5 0.9 copy-done
  115.4 0.0 copy-start.1
  115.4 47.9 %shard_map.87 = (bf16[16,8192]{1,0:T(8,128)(2,1)S(1)}, bf16[8192,2,128]{2,1,0:T(2,128)(2,1)}) custom-call(bf16[4,4,32,256]{3,2,1,0:T(8,128)(2,1)S(1)} %bitcast.9, bf16[3,512,2048]{2,1,0:T(8,128)(2,1)} %get-tuple-element.15.others_ref, bf16[2,512,2048]{2,1,0:T(8,128)(2,1)} %get-tuple-element.12.all_ref, ...), custom_call_target="tpu_custom_call" | custom-call | tf_op jit(solution)/shard_map/pallas_call | solution.py:570
  163.3 0.0 copy-done.1
  163.3 0.0 copy-start.2
  163.3 3.7 %copy.15 = bf16[1,1,3584,1024]{3,2,1,0:T(8,128)(2,1)} copy(bf16[1,1,3584,1024]{3,2,1,0:T(8,128)(2,1)S(1)} %bitcast.14) | data formatting | bytes 14680064
  167.1 0.7 copy.16
  167.8 0.5 copy-done.2
  168.3 2.0 %copy.17 = bf16[1,8192,1,2,128]{4,3,2,1,0:T(2,128)(2,1)} copy(bf16[1,8192,1,2,128]{4,3,2,1,0:T(2,128)(2,1)S(1)} %bitcast.17) | data formatting | bytes 8388608
Async XLA Ops:
  114.5 1.0 copy-start
  115.4 47.9 %copy-start.1 = (bf16[3584,1024]{1,0:T(8,128)(2,1)S(1)}, bf16[3584,1024]{1,0:T(8,128)(2,1)}, u32[]{:S(2)}) copy-start(bf16[3584,1024]{1,0:T(8,128)(2,1)} %get-tuple-element.13) | copy-start | bytes 22020100
  163.3 4.9 %copy-start.2 = (bf16[8192,2,128]{2,1,0:T(2,128)(2,1)S(1)}, bf16[8192,2,128]{2,1,0:T(2,128)(2,1)}, u32[]{:S(2)}) copy-start(bf16[8192,2,128]{2,1,0:T(2,128)(2,1)} %get-tuple-element.18) | copy-start | bytes 12582916

commit v2 on v1

--- a/solution.py
+++ b/solution.py
@@ -104,7 +104,7 @@
 def ag_kernel(np_, tiles_ref, w_ref, kv_ref, out_ref, buf, raw, wide, acc, send_sem, recv_sem, loc_sem):
     zyx = place()
     dp = lax.axis_index("dp")
-    init, events, _, _ = gather_plan(PARTS[np_], latency=0.7)
+    init, events, _, _ = gather_plan(PARTS[np_], latency=1.1)
     cols = COLS[np_]
     mine = row_of(zyx, (0, 0, 0))
     loc = pltpu.make_async_copy(tiles_ref.at[0], buf.at[pl.ds(pl.multiple_of(mine * 16, 16), 16)], loc_sem.at[0])
@@ -170,7 +170,7 @@
 
 
 def nsends(np_):
-    init, events, _, _ = gather_plan(PARTS[np_], latency=0.7)
+    init, events, _, _ = gather_plan(PARTS[np_], latency=1.1)
     return len(init) + sum(len(e[3]) for e in events)
 
 
@@ -426,6 +426,7 @@
         return pltpu.make_async_remote_copy(
             src_ref=src, dst_ref=dst, send_sem=ss, recv_sem=rs_, device_id=dev, device_id_type=MESH)
 
+    hello_all(zyx)
     loads = [pltpu.make_async_copy(pair_ref, pr.at[0], l_sem.at[0]),
              pltpu.make_async_copy(all_ref.at[0], gq.at[0], l_sem.at[1]),
              pltpu.make_async_copy(others_ref.at[2], gq.at[1], l_sem.at[2]),
@@ -438,7 +439,6 @@
             loads.append(pltpu.make_async_copy(wz_ref.at[h, k], wv.at[h, k], l_sem.at[5 + h * 4 + k]))
     for c in loads:
         c.start()
-    hello_all(zyx)
     all_said_hello()
     sends = []
 
@@ -494,8 +494,7 @@
     for c in loads[5:]:
         c.wait()
     for e in range(2):
-        wgrad(2 * e)
-        wgrad(2 * e + 1)
+        wgrad(e)
         for h in range(2):
             for k in range(3):
                 pltpu.make_async_copy(pz[h].at[k, e], pz[h].at[k, e], s_recv.at[h, k, e]).wait()
@@ -523,6 +522,8 @@
                 go(remote(tp.at[h, e, t], rs.at[h, e, 3 - d], y_send.at[h, e, d - 1], y_recv.at[h, e, 3 - d],
                           peer(1 - h, t)))
 
+    wgrad(2)
+    wgrad(3)
     for e in range(2):
         for h in range(2):
             for s in range(3):

time: 171 us -> 172 us (level)
  no operation moved by 1% of the time
where the time goes in v2:
time: 172 us; the launch traced here: 170 us
  Pallas kernels  160 us (93%)
  local copies, waits for them, and re-layouts  7.88 us (5%)
  between operations  2.01 us (1%)
    pallas_call x1, Pallas kernels, attention(): pl.pallas_call(functools.partial(attention_kernel, steps), grid=(steps,),...  58.2 us
    pallas_call x1, Pallas kernels, gather_and_project(): pl.pallas_call(functools.partial(ag_kernel, np_), in_specs=[hbm, hbm], ou...  53.5 us
    pallas_call x1, Pallas kernels, tail(): pl.pallas_call(tail_kernel, in_specs=[pl.BlockSpec(memory_space=pltpu.HBM...  48.8 us
    unnamed x9, local copies, waits for them, and re-layouts  7.88 us

profile of v2, /device:TPU:0, one launch (start us, length us, event | category | flops | bytes accessed | tf_op | source)
XLA Modules:
  0.0 170.4 jit_solution(15416690201701512946)
XLA Ops:
  0.6 53.5 %shard_map.85 = (bf16[512,256]{1,0:T(8,128)(2,1)}, bf16[2,512,2048]{2,1,0:T(8,128)(2,1)}) custom-call(bf16[1,16,8192]{2,1,0:T(8,128)(2,1)} %tiles_ref.3, bf16[8192,2,128]{2,1,0:T(2,128)(2,1)} %bitcast.11), custom_call_target="tpu_custom_call" | custom-call | tf_op jit(solution)/shard_map/pallas_call | solution.py:180
  55.4 58.2 %shard_map.86 = (bf16[3584,1024]{1,0:T(8,128)(2,1)}, bf16[512,256]{1,0:T(8,128)(2,1)}, bf16[3,512,2048]{2,1,0:T(8,128)(2,1)}, bf16[2,4,1024,2,128]{4,3,2,1,0:T(2,128)(2,1)}) custom-call(s32[1]{0:T(128)S(6)} %copy.14.cnt_ref, f32[1]{0:T(128)S(6)} %tanh.3.fac_ref, bf16[3584,1024]{1,0:T(8,128)(2,1)} %bitcast.15, bf16[3584,1024]{1,0:T(8,128)(2,1)} %bitcast.16, ...), custom_call_target="tpu_custom_call" | custom-call | tf_op jit(solution)/shard_map/pallas_call | solution.py:399
  113.7 0.0 copy-start
  113.7 0.9 copy-done
  114.6 0.0 copy-start.1
  114.6 48.8 %shard_map.87 = (bf16[16,8192]{1,0:T(8,128)(2,1)S(1)}, bf16[8192,2,128]{2,1,0:T(2,128)(2,1)}) custom-call(bf16[4,4,32,256]{3,2,1,0:T(8,128)(2,1)S(1)} %bitcast.9, bf16[3,512,2048]{2,1,0:T(8,128)(2,1)} %get-tuple-element.15.others_ref, bf16[2,512,2048]{2,1,0:T(8,128)(2,1)} %get-tuple-element.12.all_ref, ...), custom_call_target="tpu_custom_call" | custom-call | tf_op jit(solution)/shard_map/pallas_call | solution.py:571
  163.4 0.0 copy-done.1
  163.4 0.0 copy-start.2
  163.4 3.7 %copy.15 = bf16[1,1,3584,1024]{3,2,1,0:T(8,128)(2,1)} copy(bf16[1,1,3584,1024]{3,2,1,0:T(8,128)(2,1)S(1)} %bitcast.14) | data formatting | bytes 14680064
  167.1 0.7 copy.16
  167.9 0.5 copy-done.2
  168.3 2.0 %copy.17 = bf16[1,8192,1,2,128]{4,3,2,1,0:T(2,128)(2,1)} copy(bf16[1,8192,1,2,128]{4,3,2,1,0:T(2,128)(2,1)S(1)} %bitcast.17) | data formatting | bytes 8388608
Async XLA Ops:
  113.7 1.0 copy-start
  114.6 48.8 %copy-start.1 = (bf16[3584,1024]{1,0:T(8,128)(2,1)S(1)}, bf16[3584,1024]{1,0:T(8,128)(2,1)}, u32[]{:S(2)}) copy-start(bf16[3584,1024]{1,0:T(8,128)(2,1)} %get-tuple-element.13) | copy-start | bytes 22020100
  163.4 4.9 %copy-start.2 = (bf16[8192,2,128]{2,1,0:T(2,128)(2,1)S(1)}, bf16[8192,2,128]{2,1,0:T(2,128)(2,1)}, u32[]{:S(2)}) copy-start(bf16[8192,2,128]{2,1,0:T(2,128)(2,1)} %get-tuple-element.18) | copy-start | bytes 12582916
